TPU v7x, 32 devices: a whole 2x2x4 slice. The times are simulated.
32 devices in a mesh: expert: 8 (over z, y), pipe: 4 (over x, core).
Axes of the slice: x: 2, y: 2, z: 4, core: 2. Of those that a mesh axis runs over, the one named last changes fastest.
Arguments:
- layer_input: bfloat16 [4, 2048, 7168], P('pipe', 'expert'), may hold values from -6 to 6
- output_grad: bfloat16 [4, 2048, 7168], P('pipe', 'expert'), may hold values from -6 to 6
- gate_weight: bfloat16 [4, 7168, 1024], P('pipe', None, 'expert'), may hold values from -0.0625 to 0.0625
- up_weight: bfloat16 [4, 7168, 1024], P('pipe', None, 'expert'), may hold values from -0.0625 to 0.0625
- down_weight: bfloat16 [4, 1024, 7168], P('pipe', 'expert'), may hold values from -0.1875 to 0.1875
- expert_ids: int32 [4, 2048, 8], P('pipe', 'expert'), may hold values from 0 to 255, as said below
- slots: int32 [4, 2048, 8], P('pipe', 'expert'), may hold values from 0 to 32, as said below
- combine_weights: bfloat16 [4, 2048, 8], P('pipe', 'expert'), may hold values from 0.099609375 to 0.59765625
Outputs:
- prev_grad: bfloat16 [4, 2048, 7168], P('pipe', 'expert')
- gate_grad: bfloat16 [4, 7168, 1024], P('pipe', None, 'expert')
- up_grad: bfloat16 [4, 7168, 1024], P('pipe', None, 'expert')
- down_grad: bfloat16 [4, 1024, 7168], P('pipe', 'expert')
- router_grad: float32 [4, 2048, 8], P('pipe', 'expert')
Inputs may be any that keep to these rules, and one draw needn't show every extreme that they name: `expert_ids`: each token names 8 different experts. In every section one expert below 1 is named by more than 32 tokens of every device's 256 tokens. `slots`: A token's slot for an expert counts the earlier tokens of the same device's 256 tokens that name that expert, capped at 32, which marks a dropped token.
All inputs are finite; a program needn't handle non-finite values.
Results may differ from a plain program's by a relative error of at most 0.015.
Values may be sent and summed in bfloat16 or wider, within the bound.
A program may use at most 128 MiB of HBM per device.

v0:
```python
import jax
import jax.numpy as jnp
from jax import lax
from jax.sharding import PartitionSpec as P

GROUP = 8
CAP = 32


def from_behind(x, axis, by):
    size = lax.axis_size(axis)
    pairs = [(i, i + by) for i in range(size) if 0 <= i + by < size]
    return lax.ppermute(x, axis, pairs)


def shards(
    layer_input,
    output_grad,
    gate_weight,
    up_weight,
    down_weight,
    expert_ids,
    slots,
    combine_weights,
):
    devices = lax.axis_size("expert")
    window = devices // GROUP
    width = layer_input.shape[2]
    inputs = layer_input[0]
    upstream_grad = output_grad[0]
    w_gate = gate_weight[0]
    w_up = up_weight[0]
    w_down = down_weight[0]
    routes = expert_ids[0]
    places = slots[0]
    positions = routes * CAP + places
    usable = (routes < window) & (places < CAP)
    columns = lax.broadcasted_iota(jnp.int32, (1, 1, window * CAP), 2)
    picker = ((positions[:, :, None] == columns) & usable[:, :, None]).astype(jnp.float32)
    selection = jnp.sum(picker, axis=1)
    select_half = selection.astype(jnp.bfloat16)
    contract_first = (((0,), (0,)), ((), ()))
    contract_last = (((1,), (1,)), ((), ()))
    token_buffer = lax.dot_general(
        select_half, inputs, contract_first, preferred_element_type=jnp.float32
    ).astype(jnp.bfloat16)
    grad_buffer = lax.dot_general(
        select_half, upstream_grad, contract_first, preferred_element_type=jnp.float32
    ).astype(jnp.bfloat16)
    weight_buffer = jnp.einsum("tkp,tk->p", picker, combine_weights[0].astype(jnp.float32)).astype(
        jnp.bfloat16
    )
    token_blocks = token_buffer.reshape(window, CAP, width)
    grad_blocks = grad_buffer.reshape(window, CAP, width)
    weight_blocks = weight_buffer.reshape(window, CAP)
    collected = (
        lax.all_gather(token_blocks, "expert", axis=0, tiled=True),
        lax.all_gather(grad_blocks, "expert", axis=0, tiled=True),
        lax.all_gather(weight_blocks, "expert", axis=0, tiled=True),
    )
    owner = lax.axis_index("expert") // GROUP
    expert_rows = lax.dynamic_index_in_dim(
        collected[0].reshape(devices, window, CAP, width), owner, 1, False
    )
    expert_grads = lax.dynamic_index_in_dim(
        collected[1].reshape(devices, window, CAP, width), owner, 1, False
    )
    expert_weights = lax.dynamic_index_in_dim(
        collected[2].reshape(devices, window, CAP), owner, 1, False
    )
    flat_rows = expert_rows.reshape(devices * CAP, width)
    flat_grads = expert_grads.reshape(devices * CAP, width)
    flat_weights = expert_weights.reshape(devices * CAP, 1)
    gate_pre = jnp.dot(flat_rows, w_gate, preferred_element_type=jnp.float32)
    up_pre = jnp.dot(flat_rows, w_up, preferred_element_type=jnp.float32)
    sigmoid_gate = jax.nn.sigmoid(gate_pre)
    silu_gate = gate_pre * sigmoid_gate
    hidden = (silu_gate * up_pre).astype(jnp.bfloat16)
    scaled = (flat_weights.astype(jnp.float32) * flat_grads.astype(jnp.float32)).astype(
        jnp.bfloat16
    )
    partial_out = jnp.dot(hidden, w_down, preferred_element_type=jnp.float32)
    score_part = jnp.sum(partial_out * flat_grads.astype(jnp.float32), axis=1)
    back_hidden = lax.dot_general(scaled, w_down, contract_last, preferred_element_type=jnp.float32)
    dgate = (back_hidden * up_pre * sigmoid_gate * (1.0 + gate_pre * (1.0 - sigmoid_gate))).astype(
        jnp.bfloat16
    )
    dup = (back_hidden * silu_gate).astype(jnp.bfloat16)
    down_grad = lax.dot_general(
        hidden, scaled, contract_first, preferred_element_type=jnp.float32
    ).astype(jnp.bfloat16)
    gate_grad = lax.dot_general(
        flat_rows, dgate, contract_first, preferred_element_type=jnp.float32
    ).astype(jnp.bfloat16)
    up_grad = lax.dot_general(
        flat_rows, dup, contract_first, preferred_element_type=jnp.float32
    ).astype(jnp.bfloat16)
    back_input = lax.dot_general(dgate, w_gate, contract_last, preferred_element_type=jnp.float32)
    back_input = back_input + lax.dot_general(
        dup, w_up, contract_last, preferred_element_type=jnp.float32
    )
    back_half = back_input.astype(jnp.bfloat16)
    owner = lax.axis_index("expert") // GROUP
    placing = (lax.broadcasted_iota(jnp.int32, (1, window, 1), 1) == owner).astype(jnp.float32)
    back_terms = (
        back_half.reshape(devices, 1, CAP, width) * placing.astype(jnp.bfloat16)[:, :, :, None]
    )
    score_terms = score_part.reshape(devices, 1, CAP) * placing
    summed, score_summed = (
        lax.psum_scatter(back_terms, "expert", scatter_dimension=0, tiled=True).astype(jnp.float32),
        lax.psum_scatter(
            score_terms.astype(jnp.bfloat16), "expert", scatter_dimension=0, tiled=True
        ).astype(jnp.float32),
    )
    grouped = summed.reshape(window * CAP, width)
    score_sum = score_summed.reshape(window * CAP)
    contribution = jnp.dot(selection, grouped, precision=lax.Precision.HIGHEST)
    input_grad = (upstream_grad.astype(jnp.float32) + contribution).astype(jnp.bfloat16)
    router_grad = jnp.einsum("tkp,p->tk", picker, score_sum, precision=lax.Precision.HIGHEST)
    previous = from_behind(input_grad[None], "pipe", -1)
    return (previous, gate_grad[None], up_grad[None], down_grad[None], router_grad[None])


def solution(mesh):
    return jax.shard_map(
        shards,
        mesh=mesh,
        in_specs=(
            P("pipe", "expert", None),
            P("pipe", "expert", None),
            P("pipe", None, "expert"),
            P("pipe", None, "expert"),
            P("pipe", "expert", None),
            P("pipe", "expert", None),
            P("pipe", "expert", None),
            P("pipe", "expert", None),
        ),
        out_specs=(
            P("pipe", "expert", None),
            P("pipe", None, "expert"),
            P("pipe", None, "expert"),
            P("pipe", "expert", None),
            P("pipe", "expert", None),
        ),
        check_vma=False,
    )
```

profile of v0, /device:TPU:17, one launch (start us, length us, event | category | flops | bytes accessed | tf_op | source)
XLA Modules:
  0.0 319.6 jit_solution(18233484642048177575)
XLA Ops:
  7.2 0.8 and_bitcast_fusion
  8.1 0.7 add_bitcast_fusion
  8.8 0.1 convert_reduce_fusion
  8.9 3.6 %convolution_convert_fusion.3 = bf16[32,7168]{1,0:T(8,128)(2,1)} fusion(bf16[1,256,7168]{2,1,0:T(8,128)(2,1)} %param.8, f32[256,32]{0,1:T(8,128)S(1)} %convert_reduce_fusion), kind=kOutput, calls=%fused_computation.13 | convolution fusion | flops 117678080 | bytes 4161536 | tf_op jit(solution)/shard_map/dot_general | solution.py:44
  12.5 3.5 %convolution_convert_fusion.4 = bf16[32,7168]{1,0:T(8,128)(2,1)} fusion(bf16[1,256,7168]{2,1,0:T(8,128)(2,1)} %param.9, f32[256,32]{0,1:T(8,128)S(1)} %convert_reduce_fusion), kind=kOutput, calls=%fused_computation.14 | convolution fusion | flops 117678080 | bytes 4161536 | tf_op jit(solution)/shard_map/dot_general | solution.py:47
  16.1 0.0 reduce-scatter.3.cloned.1.call-start
  16.2 0.6 fusion.40
  17.4 0.2 fusion.22
  17.6 0.2 dynamic-update-slice
  17.8 61.4 %all-gather.8.cloned.1.call-done = bf16[256,7168]{1,0:T(8,128)(2,1)} async-done(((bf16[32,7168]{1,0:T(8,128)(2,1)}), bf16[256,7168]{1,0:T(8,128)(2,1)}) %all-gather.8.cloned.1.call-update) | async-done | bytes 3670032 | tf_op jit(solution)/shard_map/all_gather | solution.py:57
  79.2 3.9 %fusion.14 = f32[256,128]{1,0:T(8,128)S(1)} fusion(bf16[256,7168]{1,0:T(8,128)(2,1)} %all-gather.8.cloned.1.call-done, bf16[1,7168,128]{2,1,0:T(8,128)(2,1)} %param.10), kind=kOutput, calls=%fused_computation.24 | convolution fusion | flops 469762048 | bytes 5636096 | tf_op jit(solution)/shard_map/dot_general | solution.py:74
  83.0 1.2 multiply_convert_fusion.3
  84.2 63.0 %all-gather.6.cloned.1.call-done = bf16[256,7168]{1,0:T(8,128)(2,1)} async-done(((bf16[32,7168]{1,0:T(8,128)(2,1)}), bf16[256,7168]{1,0:T(8,128)(2,1)}) %all-gather.6.cloned.1.call-update) | async-done | bytes 3670032 | tf_op jit(solution)/shard_map/all_gather | solution.py:58
  147.2 3.8 %fusion.11 = f32[256]{0:T(256)S(1)} fusion(bf16[256,7168]{1,0:T(8,128)(2,1)} %all-gather.6.cloned.1.call-done, bf16[256,128]{1,0:T(8,128)(2,1)S(1)} %get-tuple-element.11, bf16[1,128,7168]{2,1,0:T(8,128)(2,1)} %param.12), kind=kOutput, calls=%fused_computation.21 | convolution fusion | flops 475266816 | bytes 5571584 | tf_op jit(solution)/shard_map/dot_general | solution.py:82
  151.0 0.1 convert_element_type.125
  151.1 11.1 %all-reduce.2 = (bf16[256]{0:T(256)(128)(2,1)S(1)}, bf16[8,1,32]{2,0,1:T(8,128)(2,1)S(1)}) all-reduce(bf16[256]{0:T(256)(128)(2,1)S(1)} %dynamic-update-slice, bf16[8,1,32]{2,0,1:T(8,128)(2,1)S(1)} %convert_element_type.125), channel_id=2, replica_groups=mesh['expert'=8,'pipe'=4] {'expert'}, use_global_device_ids=true, to_apply=%add | all-reduce | flops 512 | bytes 2048
  162.2 0.1 reshape.145
  162.2 3.1 multiply_convert_fusion.1
  165.4 1.1 multiply_convert_fusion.4
  166.5 0.4 copy-done.4
  166.9 1.1 fusion.12
  168.0 3.0 fusion.3
  171.0 87.2 %reduce-scatter.3.cloned.1.call-done = bf16[1,1,32,7168]{3,2,0,1:T(8,128)(2,1)} async-done(((bf16[8,1,32,7168]{3,2,0,1:T(8,128)(2,1)}), bf16[1,1,32,7168]{3,2,0,1:T(8,128)(2,1)}) %reduce-scatter.3.cloned.1.call-update) | async-done | bytes 458768 | tf_op jit(solution)/shard_map/reduce_scatter | solution.py:110
  258.2 6.3 %fusion.2 = bf16[1,256,7168]{2,1,0:T(8,128)(2,1)} fusion(f32[256,32]{0,1:T(8,128)S(1)} %convert_reduce_fusion, bf16[1,256,7168]{2,1,0:T(8,128)(2,1)} %param.9, bf16[1,1,32,7168]{3,2,0,1:T(8,128)(2,1)} %reduce-scatter.3.cloned.1.call-done), kind=kOutput, calls=%fused_computation.5 | convolution fusion | flops 710148096 | bytes 7831552 | tf_op jit(solution)/shard_map/dot_general | solution.py:117
  264.4 2.7 collective-permute-start
  267.1 1.0 fusion.27
  268.1 0.9 copy.20
  269.0 4.6 %fusion.5 = bf16[1,7168,128]{2,1,0:T(8,128)(2,1)} fusion(bf16[256,7168]{1,0:T(8,128)(2,1)} %all-gather.8.cloned.1.call-done, bf16[256,128]{1,0:T(8,128)(2,1)S(1)} %get-tuple-element.7), kind=kOutput, calls=%fused_computation.11 | convolution fusion | flops 470679552 | bytes 5570560 | tf_op jit(solution)/shard_map/dot_general | solution.py:95
  273.6 2.4 fusion.4
  276.0 2.3 fusion.6
  278.4 30.6 %collective-permute-done = bf16[1,256,7168]{2,1,0:T(8,128)(2,1)} collective-permute-done((bf16[1,256,7168]{2,1,0:T(8,128)(2,1)}, bf16[1,256,7168]{2,1,0:T(8,128)(2,1)}, u32[]{:S(2)}, u32[]{:S(2)}) %collective-permute-start) | collective-permute-done | bytes 3670048 | tf_op jit(solution)/shard_map/ppermute | solution.py:13
  308.9 4.1 %copy.27 = bf16[1,256,7168]{2,1,0:T(8,128)(2,1)} copy(bf16[1,256,7168]{2,1,0:T(8,128)(2,1)} %collective-permute-done) | data formatting | bytes 7340032
  (23 shorter events, 0.2 us)
Async XLA Ops:
  7.2 75.9 %copy-start = (bf16[1,7168,128]{2,1,0:T(8,128)(2,1)S(1)}, bf16[1,7168,128]{2,1,0:T(8,128)(2,1)}, u32[]{:S(2)}) copy-start(bf16[1,7168,128]{2,1,0:T(8,128)(2,1)} %param.11) | copy-start | bytes 5505028
  7.2 72.0 %all-gather.8.cloned.1.call-start = ((), (), s32[]{:S(2)}) async-start(), calls=%async_computation.3 | async-start | bytes 4128768 | tf_op jit(solution)/shard_map/all_gather | solution.py:57
  8.8 7.3 %copy-start.5 = (u32[32]{0:T(128)S(1)}, u32[32]{0:T(128)}, u32[]{:S(2)}) copy-start(u32[32]{0:T(128)} %constant.53) | copy-start | bytes 388
  8.9 8.5 %copy-start.7 = (bf16[1,256,8]{1,2,0:T(8,128)(2,1)S(1)}, bf16[1,256,8]{1,2,0:T(8,128)(2,1)}, u32[]{:S(2)}) copy-start(bf16[1,256,8]{1,2,0:T(8,128)(2,1)} %param.15) | copy-start | bytes 12292
  12.4 134.8 %all-gather.6.cloned.1.call-start = ((), (), s32[]{:S(2)}) async-start(), calls=%async_computation.2 | async-start | bytes 4128768 | tf_op jit(solution)/shard_map/all_gather | solution.py:58
  16.1 242.1 %reduce-scatter.3.cloned.1.call-start = ((), (), s32[]{:S(2)}) async-start(), calls=%async_computation.1 | async-start | bytes 4128768 | tf_op jit(solution)/shard_map/reduce_scatter | solution.py:110
  79.2 3.9 %copy-start.1 = (bf16[256,7168]{1,0:T(8,128)(2,1)S(1)}, bf16[256,7168]{1,0:T(8,128)(2,1)}, u32[]{:S(2)}) copy-start(bf16[256,7168]{1,0:T(8,128)(2,1)} %all-gather.8.cloned.1.call-done) | copy-start | bytes 11010052
  162.2 3.1 copy-start.6
  165.4 1.5 copy-start.4
  264.4 44.5 %collective-permute-start = (bf16[1,256,7168]{2,1,0:T(8,128)(2,1)}, bf16[1,256,7168]{2,1,0:T(8,128)(2,1)}, u32[]{:S(2)}, u32[]{:S(2)}) collective-permute-start(bf16[1,256,7168]{2,1,0:T(8,128)(2,1)} %fusion.2), channel_id=1, source_target_pairs={{1,0},{2,1},{3,2},{5,4},{6,5},{7,6},{9,8},{10,9},{11,10},{13,12},{... | collective-permute-start | bytes 11010056 | tf_op jit(solution)/shard_map/ppermute | solution.py:13
  269.0 4.6 %copy-start.2 = (bf16[256,7168]{1,0:T(8,128)(2,1)S(1)}, bf16[256,7168]{1,0:T(8,128)(2,1)}, u32[]{:S(2)}) copy-start(bf16[256,7168]{1,0:T(8,128)(2,1)} %all-gather.8.cloned.1.call-done) | copy-start | bytes 11010052
  273.6 2.4 copy-start.3
Sparse Core Ops, SparseCore 0:
  12.6 66.5 all-gather.7
  81.9 65.2 all-gather.5
  171.1 86.9 reduce-scatter.2
where the time goes:
time: 321 us; the launch traced here: 320 us
  waiting for transfers between devices  242 us (75%)
  matrix products  37.9 us (12%)
  between operations  14.6 us (5%)
  blocking collectives  11.1 us (3%)
  local copies, waits for them, and re-layouts  6.39 us (2%)
  other arithmetic  4.73 us (1%)
    reduce_scatter x1, waiting for transfers between devices, shards(): lax.psum_scatter(back_terms, 'expert', scatter_dimension=0, tiled=True)  87.2 us
    all_gather x1, waiting for transfers between devices, shards(): lax.all_gather(grad_blocks, 'expert', axis=0, tiled=True)  63 us
    all_gather x1, waiting for transfers between devices, shards(): lax.all_gather(token_blocks, 'expert', axis=0, tiled=True)  61.4 us
    ppermute x1, waiting for transfers between devices, from_behind(): return lax.ppermute(x, axis, pairs)  30.6 us
    unnamed x1, blocking collectives  11.1 us
  transfers between devices with their start and end apart: 4, of which 4 were waited for; matrix products, arithmetic and copies ran while one was open for 7% of the time, Pallas kernels for 0%

commit v1 on v0

--- a/solution.py
+++ b/solution.py
@@ -1,10 +1,16 @@
+import functools
+
 import jax
 import jax.numpy as jnp
 from jax import lax
+from jax.experimental import pallas as pl
+from jax.experimental.pallas import tpu as pltpu
 from jax.sharding import PartitionSpec as P
 
 GROUP = 8
 CAP = 32
+COLS = 2
+MESH = pl.DeviceIdType.MESH
 
 
 def from_behind(x, axis, by):
@@ -121,9 +127,523 @@
     return (previous, gate_grad[None], up_grad[None], down_grad[None], router_grad[None])
 
 
+def cuts(width, count):
+    narrow = width // 7 // 128 * 128
+    wide = (width - narrow) // count // 128 * 128
+    pieces = [(i * wide, wide, True) for i in range(count)]
+    return pieces, (count * wide, width - count * wide, False)
+
+
+def exchange(
+    pipes,
+    wide_count,
+    layer_ref,
+    upstream_ref,
+    gate_ref,
+    up_ref,
+    down_ref,
+    select_ref,
+    weight_ref,
+    rows_out,
+    grads_out,
+    pair_out,
+    hidden_out,
+    behind_out,
+    select_out,
+    sums_out,
+    score_out,
+    layer_buf,
+    upstream_buf,
+    x_all,
+    g_all,
+    w_pair,
+    w_down,
+    part,
+    from_y,
+    from_above,
+    from_below,
+    both,
+    back,
+    temp,
+    local_sem,
+    ag_rx,
+    ag_up,
+    ag_dn,
+    ag_y,
+    rs_y_tx,
+    rs_y_rx,
+    rs_up_tx,
+    rs_up_rx,
+    rs_dn_tx,
+    rs_dn_rx,
+    pipe_tx,
+    pipe_rx,
+):
+    me = lax.axis_index("expert")
+    stage = lax.axis_index("pipe")
+    y = lax.rem(me, COLS)
+    z = lax.div(me, COLS)
+    top = GROUP // COLS - 1
+    other = 1 - y
+    partner = me + 1 - 2 * y
+    above, below = me + COLS, me - COLS
+    width = layer_ref.shape[1]
+    total = x_all.shape[0]
+    wide, narrow = cuts(width, wide_count)
+    pieces = [narrow] + wide
+    count = len(pieces)
+    not_top, not_low = z < top, z > 0
+    to_pipe, from_pipe = stage > 0, stage < pipes - 1
+
+    def rows(block):
+        return pl.ds(pl.multiple_of(block * CAP, CAP), CAP)
+
+    local = []
+
+    def load(src, dst):
+        copy = pltpu.make_async_copy(src, dst, local_sem.at[len(local)])
+        local.append(copy)
+        copy.start()
+        return copy
+
+    layer_loads = [
+        load(layer_ref.at[:, pl.ds(c, w)], layer_buf.at[:, pl.ds(c, w)]) for c, w, _ in pieces
+    ]
+    upstream_loads = [
+        load(upstream_ref.at[:, pl.ds(c, w)], upstream_buf.at[:, pl.ds(c, w)]) for c, w, _ in pieces
+    ]
+    weight_loads = [
+        load(gate_ref, w_pair.at[:, pl.ds(0, 128)]),
+        load(up_ref, w_pair.at[:, pl.ds(128, 128)]),
+        load(down_ref, w_down),
+    ]
+
+    barrier = pltpu.get_barrier_semaphore()
+    pl.semaphore_signal(barrier, inc=1, device_id={"expert": partner}, device_id_type=MESH)
+
+    @pl.when(not_top)
+    def _():
+        pl.semaphore_signal(barrier, inc=1, device_id={"expert": above}, device_id_type=MESH)
+
+    @pl.when(not_low)
+    def _():
+        pl.semaphore_signal(barrier, inc=1, device_id={"expert": below}, device_id_type=MESH)
+
+    @pl.when(to_pipe)
+    def _():
+        pl.semaphore_signal(barrier, inc=1, device_id={"pipe": stage - 1}, device_id_type=MESH)
+
+    @pl.when(from_pipe)
+    def _():
+        pl.semaphore_signal(barrier, inc=1, device_id={"pipe": stage + 1}, device_id_type=MESH)
+
+    def one(flag):
+        return jnp.where(flag, 1, 0).astype(jnp.int32)
+
+    pl.semaphore_wait(barrier, 1 + one(not_top) + one(not_low) + one(to_pipe) + one(from_pipe))
+
+    sent = []
+
+    def send(conds, src, dst, tx, rx, device):
+        def make():
+            return pltpu.make_async_remote_copy(
+                src_ref=src(),
+                dst_ref=dst(),
+                send_sem=tx(),
+                recv_sem=rx(),
+                device_id=device,
+                device_id_type=MESH,
+            )
+
+        guard(conds, lambda: make().start())
+        return conds, make
+
+    def guard(conds, run):
+        if conds:
+            flag = conds[0]
+            for cond in conds[1:]:
+                flag = flag & cond
+            pl.when(flag)(run)
+        else:
+            run()
+
+    def arrived(ref, tx, rx):
+        pltpu.make_async_remote_copy(
+            src_ref=ref,
+            dst_ref=ref,
+            send_sem=tx,
+            recv_sem=rx,
+            device_id={"expert": partner},
+            device_id_type=MESH,
+        ).wait_recv()
+
+    messages = []
+    for array in (x_all, g_all):
+        for c, w, is_wide in pieces:
+            if array is g_all and not is_wide:
+                w = w + 128
+            messages.append((array, c, w, is_wide, len(messages)))
+
+    def gather_send(message, block, conds, tx, device):
+        array, c, w, _, n = message
+        view = lambda: array.at[rows(block), pl.ds(c, w)]
+        return send(
+            conds, view, view, lambda: tx.at[block, n], lambda: ag_rx.at[block, n], device
+        )
+
+    def gather_wait(message, block):
+        array, c, w, _, n = message
+        arrived(array.at[rows(block), pl.ds(c, w)], ag_y.at[block, n], ag_rx.at[block, n])
+
+    to_above = {"expert": above}
+    to_below = {"expert": below}
+    to_partner = {"expert": partner}
+
+    picked = select_ref[...]
+    g_all[rows(me), pl.ds(width, 128)] = weight_ref[...]
+    for message in messages:
+        array, c, w, is_wide, n = message
+        at = n % count
+        loads, source = (
+            (layer_loads, layer_buf) if array is x_all else (upstream_loads, upstream_buf)
+        )
+        span = pieces[at][1]
+        loads[at].wait()
+        array[rows(me), pl.ds(c, span)] = jnp.dot(
+            picked, source[:, pl.ds(c, span)], preferred_element_type=jnp.float32
+        ).astype(jnp.bfloat16)
+        sent.append(gather_send(message, me, [], ag_y, to_partner))
+        sent.append(gather_send(message, me, [not_top], ag_up, to_above))
+        sent.append(gather_send(message, me, [not_low], ag_dn, to_below))
+
+    to_prev = {"pipe": stage - 1}
+    sent.append(
+        send(
+            [to_pipe],
+            lambda: select_ref,
+            lambda: select_out,
+            lambda: pipe_tx.at[0],
+            lambda: pipe_rx.at[0],
+            to_prev,
+        )
+    )
+    sent.append(
+        send(
+            [to_pipe],
+            lambda: upstream_ref,
+            lambda: behind_out,
+            lambda: pipe_tx.at[1],
+            lambda: pipe_rx.at[1],
+            to_prev,
+        )
+    )
+
+    beside = z * COLS + other
+    for message in messages:
+        if not message[3]:
+            gather_wait(message, beside)
+            sent.append(gather_send(message, beside, [not_top], ag_up, to_above))
+            sent.append(gather_send(message, beside, [not_low], ag_dn, to_below))
+
+    for k in range(1, top + 1):
+        for message in messages:
+            for low in (True, False):
+                at_z = z - k if low else z + k
+                valid = z >= k if low else z + k <= top
+                onward, tx, device = (
+                    (not_top, ag_up, to_above) if low else (not_low, ag_dn, to_below)
+                )
+                for column in [y] if message[3] else [y, other]:
+                    block = at_z * COLS + column
+                    guard([valid], functools.partial(gather_wait, message, block))
+                    sent.append(gather_send(message, block, [valid, onward], tx, device))
+                    if message[3]:
+                        sent.append(gather_send(message, block, [valid], ag_y, to_partner))
+    for message in messages:
+        if message[3]:
+            for at_z in range(top + 1):
+                gather_wait(message, at_z * COLS + other)
+
+    for copy in weight_loads:
+        copy.wait()
+    rows_copy = load(x_all, rows_out)
+    grads_copy = load(g_all.at[:, pl.ds(0, width)], grads_out)
+    step = width // 7
+    both[...] = jnp.zeros_like(both)
+    back[...] = jnp.zeros_like(back)
+
+    def forward(i, _):
+        at = pl.ds(pl.multiple_of(i * step, 128), step)
+        both[...] += jnp.dot(x_all[:, at], w_pair[at, :], preferred_element_type=jnp.float32)
+        back[...] += lax.dot_general(
+            g_all[:, at],
+            w_down[:, at],
+            (((1,), (1,)), ((), ())),
+            preferred_element_type=jnp.float32,
+        )
+        return 0
+
+    lax.fori_loop(0, 7, forward, 0)
+    gate = both[:, pl.ds(0, 128)]
+    up = both[:, pl.ds(128, 128)]
+    raw = back[...]
+    scale = g_all[:, pl.ds(width, 128)].astype(jnp.float32)
+    sigmoid = jax.nn.sigmoid(gate)
+    silu = gate * sigmoid
+    hidden = (silu * up).astype(jnp.bfloat16).astype(jnp.float32)
+    score = jnp.sum(hidden * raw, axis=1, keepdims=True)
+    part[:, pl.ds(width, 128)] = jnp.broadcast_to(score, (total, 128)).astype(jnp.bfloat16)
+    scaled = scale * raw
+    pair_out[:, pl.ds(0, 128)] = (
+        scaled * up * sigmoid * (1.0 + gate * (1.0 - sigmoid))
+    ).astype(jnp.bfloat16)
+    pair_out[:, pl.ds(128, 128)] = (scaled * silu).astype(jnp.bfloat16)
+    hidden_out[...] = (hidden * scale).astype(jnp.bfloat16)
+
+    def part_view(buffer, block, n):
+        c, w, is_wide = pieces[n]
+        return buffer.at[rows(block), pl.ds(c, w if is_wide else w + 128)]
+
+    def part_send(n, block, conds, buffer, tx, rx, device):
+        return send(
+            conds,
+            lambda: part_view(part, block, n),
+            lambda: part_view(buffer, block, n),
+            lambda: tx.at[block, n],
+            lambda: rx.at[block, n],
+            device,
+        )
+
+    def part_wait(n, block, buffer, tx, rx):
+        arrived(part_view(buffer, block, n), tx.at[block, n], rx.at[block, n])
+
+    def order(run):
+        for k in range(top, 0, -1):
+            run(z - k, z >= k)
+            run(z + k, z + k <= top)
+        run(z, None)
+
+    for n, (c, w, is_wide) in enumerate(pieces):
+        for start in range(c, c + w, 1024):
+            at = pl.ds(start, min(1024, c + w - start))
+            part[:, at] = lax.dot_general(
+                pair_out[...],
+                w_pair[at, :],
+                (((1,), (1,)), ((), ())),
+                preferred_element_type=jnp.float32,
+            ).astype(jnp.bfloat16)
+        if is_wide:
+            order(
+                lambda at_z, valid, n=n: sent.append(
+                    part_send(
+                        n,
+                        at_z * COLS + other,
+                        [] if valid is None else [valid],
+                        from_y,
+                        rs_y_tx,
+                        rs_y_rx,
+                        to_partner,
+                    )
+                )
+            )
+
+    def merge(n, block, terms):
+        c, w, is_wide = pieces[n]
+        w = w if is_wide else w + 128
+        here = (rows(block), pl.ds(c, w))
+        temp[:, pl.ds(0, w)] = part[here].astype(jnp.float32)
+        for cond, buffer, tx, rx in terms:
+
+            def add(buffer=buffer, tx=tx, rx=rx):
+                part_wait(n, block, buffer, tx, rx)
+                temp[:, pl.ds(0, w)] += buffer[here].astype(jnp.float32)
+
+            guard([] if cond is None else [cond], add)
+        part[here] = temp[:, pl.ds(0, w)].astype(jnp.bfloat16)
+
+    via_y = (None, from_y, rs_y_tx, rs_y_rx)
+    via_above = (not_top, from_above, rs_dn_tx, rs_dn_rx)
+    via_below = (not_low, from_below, rs_up_tx, rs_up_rx)
+    for k in range(top, 0, -1):
+        for n in range(count):
+            for low in (True, False):
+                at_z = z - k if low else z + k
+                valid = z >= k if low else z + k <= top
+                is_wide = pieces[n][2]
+                for column in [y] if is_wide else [y, other]:
+                    block = at_z * COLS + column
+                    terms = ([via_y] if is_wide else []) + [via_above if low else via_below]
+                    guard([valid], functools.partial(merge, n, block, terms))
+                    if low:
+                        out = (from_above, rs_dn_tx, rs_dn_rx, to_below)
+                    else:
+                        out = (from_below, rs_up_tx, rs_up_rx, to_above)
+                    sent.append(part_send(n, block, [valid], *out))
+    for n in range(count):
+        c, w, is_wide = pieces[n]
+        if is_wide:
+            merge(n, me, [via_y, via_above, via_below])
+        else:
+            merge(n, beside, [via_above, via_below])
+            sent.append(part_send(n, beside, [], from_y, rs_y_tx, rs_y_rx, to_partner))
+            merge(n, me, [via_above, via_below, via_y])
+        sent.append(
+            send(
+                [to_pipe],
+                lambda c=c, w=w: part.at[rows(me), pl.ds(c, w)],
+                lambda c=c, w=w: sums_out.at[:, pl.ds(c, w)],
+                lambda n=n: pipe_tx.at[2 + n],
+                lambda n=n: pipe_rx.at[2 + n],
+                to_prev,
+            )
+        )
+    score_out[...] = part[rows(me), pl.ds(width, 128)].astype(jnp.float32)
+
+    @pl.when(from_pipe)
+    def _():
+        arrived(select_out, pipe_tx.at[0], pipe_rx.at[0])
+        arrived(behind_out, pipe_tx.at[1], pipe_rx.at[1])
+        for n, (c, w, _) in enumerate(pieces):
+            arrived(sums_out.at[:, pl.ds(c, w)], pipe_tx.at[2 + n], pipe_rx.at[2 + n])
+
+    for conds, make in sent:
+        guard(conds, lambda make=make: make().wait_send())
+    rows_copy.wait()
+    grads_copy.wait()
+
+
+def finish(
+    keep, x, g, pair, hidden, behind, select, sums, prev_out, gate_out, up_out, down_out
+):
+    first = (((0,), (0,)), ((), ()))
+    grads = lax.dot_general(x[...], pair[...], first, preferred_element_type=jnp.float32)
+    gate_out[...] = grads[:, :128].astype(jnp.bfloat16)
+    up_out[...] = grads[:, 128:].astype(jnp.bfloat16)
+    down_out[...] = lax.dot_general(
+        hidden[...], g[...], first, preferred_element_type=jnp.float32
+    ).astype(jnp.bfloat16)
+    moved = lax.dot_general(select[...], sums[...], first, preferred_element_type=jnp.float32)
+    prev = behind[...].astype(jnp.float32) + moved
+    prev_out[...] = jnp.where(keep[0] > 0, prev, 0.0).astype(jnp.bfloat16)
+
+
+def fused(
+    pipes,
+    layer_input,
+    output_grad,
+    gate_weight,
+    up_weight,
+    down_weight,
+    expert_ids,
+    slots,
+    combine_weights,
+):
+    _, tokens, width = layer_input.shape
+    half = jnp.bfloat16
+    units = gate_weight.shape[2]
+    total = GROUP * CAP
+    routes, places = expert_ids[0], slots[0]
+    usable = (routes < 1) & (places < CAP)
+    positions = jnp.where(usable, routes * CAP + places, CAP)
+    hits = positions.T[:, None, :] == lax.broadcasted_iota(jnp.int32, (1, CAP, 1), 1)
+    select = jnp.sum(hits.astype(jnp.float32), axis=0).astype(half)
+    weight = jnp.sum(
+        jnp.where(hits, combine_weights[0].astype(jnp.float32).T[:, None, :], 0.0), axis=(0, 2)
+    )
+    weight = jnp.broadcast_to(weight.astype(half)[:, None], (CAP, 128))
+    wide_count = 3
+    wide, narrow = cuts(width, wide_count)
+    count = len(wide) + 1
+    widest = max([w for _, w, _ in wide] + [narrow[1] + 128])
+    dma = pltpu.SemaphoreType.DMA
+    vmem = pl.BlockSpec(memory_space=pltpu.VMEM)
+    hbm = pl.BlockSpec(memory_space=pl.ANY)
+    shape = jax.ShapeDtypeStruct
+    x_all, g_all, pair, hidden, behind, select_next, sums, score = pl.pallas_call(
+        functools.partial(exchange, pipes, wide_count),
+        out_shape=(
+            shape((total, width), half),
+            shape((total, width), half),
+            shape((total, 2 * units), half),
+            shape((total, units), half),
+            shape((tokens, width), half),
+            shape((CAP, tokens), half),
+            shape((CAP, width), half),
+            shape((CAP, 128), jnp.float32),
+        ),
+        in_specs=[hbm, hbm, hbm, hbm, hbm, vmem, vmem],
+        out_specs=(hbm, hbm, vmem, vmem, hbm, hbm, hbm, vmem),
+        scratch_shapes=[
+            pltpu.VMEM((tokens, width), half),
+            pltpu.VMEM((tokens, width), half),
+            pltpu.VMEM((total, width), half),
+            pltpu.VMEM((total, width + 128), half),
+            pltpu.VMEM((width, 2 * units), half),
+            pltpu.VMEM((units, width), half),
+            pltpu.VMEM((total, width + 128), half),
+            pltpu.VMEM((total, width + 128), half),
+            pltpu.VMEM((total, width + 128), half),
+            pltpu.VMEM((total, width + 128), half),
+            pltpu.VMEM((total, 2 * units), jnp.float32),
+            pltpu.VMEM((total, units), jnp.float32),
+            pltpu.VMEM((CAP, widest), jnp.float32),
+            dma((2 * count + 5,)),
+            *[dma((GROUP, 2 * count)) for _ in range(4)],
+            *[dma((GROUP, count)) for _ in range(6)],
+            dma((2 + count,)),
+            dma((2 + count,)),
+        ],
+        compiler_params=pltpu.CompilerParams(
+            collective_id=0, has_side_effects=True, vmem_limit_bytes=50 * 1024 * 1024
+        ),
+        name="exchange",
+    )(
+        layer_input[0],
+        output_grad[0],
+        gate_weight[0],
+        up_weight[0],
+        down_weight[0],
+        select,
+        weight,
+    )
+    keep = jnp.where(lax.axis_index("pipe") < pipes - 1, 1, 0).astype(jnp.int32).reshape(1)
+    tile = width // 7
+    across = lambda height: pl.BlockSpec((height, tile), lambda i: (0, i))
+    along = pl.BlockSpec((tile, units), lambda i: (i, 0))
+    whole = lambda *dims: pl.BlockSpec(dims, lambda i: (0, 0))
+    prev, gate_grad, up_grad, down_grad = pl.pallas_call(
+        finish,
+        grid=(7,),
+        out_shape=(
+            shape((tokens, width), half),
+            shape((width, units), half),
+            shape((width, units), half),
+            shape((units, width), half),
+        ),
+        in_specs=[
+            pl.BlockSpec(memory_space=pltpu.SMEM),
+            across(total),
+            across(total),
+            whole(total, 2 * units),
+            whole(total, units),
+            across(tokens),
+            whole(CAP, tokens),
+            across(CAP),
+        ],
+        out_specs=(across(tokens), along, along, across(units)),
+        compiler_params=pltpu.CompilerParams(vmem_limit_bytes=40 * 1024 * 1024),
+        name="finish",
+    )(keep, x_all, g_all, pair, hidden, behind, select_next, sums)
+    router_grad = jnp.sum(jnp.where(hits, score[:, 0][None, :, None], 0.0), axis=1).T
+    return (prev[None], gate_grad[None], up_grad[None], down_grad[None], router_grad[None])
+
+
 def solution(mesh):
+    body = shards
+    if mesh.shape["expert"] == GROUP:
+        body = functools.partial(fused, mesh.shape["pipe"])
     return jax.shard_map(
-        shards,
+        body,
         mesh=mesh,
         in_specs=(
             P("pipe", "expert", None),

time: 321 us -> 162 us (0.50)
  waiting for transfers between devices: 242 us -> 0 us
  Pallas kernels: 0 us -> 151 us
  matrix products: 37.9 us -> 0 us
  between operations: 14.6 us -> 0.66 us
  blocking collectives: 11.1 us -> 0 us
    pallas_call x0 -> x2, Pallas kernels: none -> 151 us  [the longest x1 145 us: fused(): pl.pallas_call(functools.partial(exchange, pipes, wide_count), out_shape=...]
    all_gather x2 -> x0, waiting for transfers between devices: 124 us -> none  [the longest x1 63 us: shards(): lax.all_gather(grad_blocks, 'expert', axis=0, tiled=True)]
    reduce_scatter x1 -> x0, waiting for transfers between devices: 87.2 us -> none  [shards(): lax.psum_scatter(back_terms, 'expert', scatter_dimension=0, tiled=True)]
    dot_general x14 -> x0, matrix products: 37.9 us -> none  [the longest x1 6.25 us: shards(): contribution = jnp.dot(selection, grouped, precision=lax.Precision.HIGHEST)]
    ppermute x1 -> x0, waiting for transfers between devices: 30.6 us -> none  [from_behind(): return lax.ppermute(x, axis, pairs)]
    unnamed x1 -> x0, blocking collectives: 11.1 us -> none
    unnamed x20 -> x8, local copies, waits for them, and re-layouts: 5.3 us -> 7.61 us
  transfers between devices with their start and end apart: 4 -> 0, of which waited for: 4 -> 0; matrix products, arithmetic and copies ran while one was open for 7% -> 0% of each run, Pallas kernels for 0% -> 0%
where the time goes in v1:
time: 162 us
  Pallas kernels  151 us (93%)
  local copies, waits for them, and re-layouts  7.79 us (5%)
  other arithmetic  2.29 us (1%)
    pallas_call x1, Pallas kernels, fused(): pl.pallas_call(functools.partial(exchange, pipes, wide_count), out_shape=...  145 us
    unnamed x8, local copies, waits for them, and re-layouts  7.61 us
    pallas_call x1, Pallas kernels, fused(): pl.pallas_call(finish, grid=(7,), out_shape=(shape((tokens, width), half)...  6.63 us

profile of v1, /device:TPU:17, one launch (start us, length us, event | category | flops | bytes accessed | tf_op | source)
XLA Modules:
  0.0 161.9 jit_solution(17245581587815398406)
XLA Ops:
  0.6 0.7 select_bitcast_fusion
  1.4 0.7 convert_bitcast_fusion
  2.0 0.2 select_reduce_fusion.1
  2.2 0.1 broadcast_in_dim.51.weight_ref
  2.3 0.0 copy-start.3
  2.3 1.5 copy-done.3
  3.8 144.6 %exchange.1 = (bf16[256,7168]{1,0:T(8,128)(2,1)}, bf16[256,7168]{1,0:T(8,128)(2,1)}, bf16[256,256]{1,0:T(8,128)(2,1)S(1)}, bf16[256,128]{1,0:T(8,128)(2,1)S(1)},...) custom-call(bf16[256,7168]{1,0:T(8,128)(2,1)} %bitcast.23, ...), custom_call_target="tpu_custom_call" | custom-call | tf_op jit(solution)/shard_map/exchange/pallas_call | solution.py:562
  148.4 0.0 copy-start
  148.4 2.0 %copy-done = bf16[256,7168]{1,0:T(8,128)(2,1)S(1)} copy-done((bf16[256,7168]{1,0:T(8,128)(2,1)S(1)}, bf16[256,7168]{1,0:T(8,128)(2,1)}, u32[]{:S(2)}) %copy-start) | copy-done | bytes 3670040
  150.4 0.0 copy-start.1
  150.4 2.0 %copy-done.1 = bf16[256,7168]{1,0:T(8,128)(2,1)S(1)} copy-done((bf16[256,7168]{1,0:T(8,128)(2,1)S(1)}, bf16[256,7168]{1,0:T(8,128)(2,1)}, u32[]{:S(2)}) %copy-start.1) | copy-done | bytes 3670040
  152.4 0.0 copy-start.2
  152.4 2.0 %copy-done.2 = bf16[256,7168]{1,0:T(8,128)(2,1)S(1)} copy-done((bf16[256,7168]{1,0:T(8,128)(2,1)S(1)}, bf16[256,7168]{1,0:T(8,128)(2,1)}, u32[]{:S(2)}) %copy-start.2) | copy-done | bytes 3670040
  154.5 6.6 %finish.1 = (bf16[256,7168]{1,0:T(8,128)(2,1)}, bf16[7168,128]{1,0:T(8,128)(2,1)}, bf16[7168,128]{1,0:T(8,128)(2,1)}, bf16[128,7168]{1,0:T(8,128)(2,1)}) custom-call(s32[1]{0:T(128)} %bitcast.keep, bf16[256,7168]{1,0:T(8,128)(2,1)S(1)} %copy-done, bf16[256,7168]{1,0:T(8,128)(2,1)S(1)} %copy-done.1, bf16[256,256]{1,0:T(8,128)(2,1)S(1)} %get-tuple-element.19.pair, ...), custom_call_target="tpu_custom_call" | custom-call | tf_op jit(solution)/shard_map/finish/pallas_call | solution.py:614
  161.1 0.1 slice_reduce_fusion
  161.2 0.7 select_reduce_fusion
Async XLA Ops:
  2.3 1.5 copy-start.3
  148.4 2.0 %copy-start = (bf16[256,7168]{1,0:T(8,128)(2,1)S(1)}, bf16[256,7168]{1,0:T(8,128)(2,1)}, u32[]{:S(2)}) copy-start(bf16[256,7168]{1,0:T(8,128)(2,1)} %get-tuple-element.17.x) | copy-start | bytes 11010052
  150.4 2.0 %copy-start.1 = (bf16[256,7168]{1,0:T(8,128)(2,1)S(1)}, bf16[256,7168]{1,0:T(8,128)(2,1)}, u32[]{:S(2)}) copy-start(bf16[256,7168]{1,0:T(8,128)(2,1)} %get-tuple-element.18.g) | copy-start | bytes 11010052
  152.4 2.0 %copy-start.2 = (bf16[256,7168]{1,0:T(8,128)(2,1)S(1)}, bf16[256,7168]{1,0:T(8,128)(2,1)}, u32[]{:S(2)}) copy-start(bf16[256,7168]{1,0:T(8,128)(2,1)} %get-tuple-element.21.behind) | copy-start | bytes 11010052

commit v2 on v1

--- a/solution.py
+++ b/solution.py
@@ -10,6 +10,7 @@
 GROUP = 8
 CAP = 32
 COLS = 2
+HALF = CAP // 2
 MESH = pl.DeviceIdType.MESH
 
 
@@ -127,16 +128,28 @@
     return (previous, gate_grad[None], up_grad[None], down_grad[None], router_grad[None])
 
 
-def cuts(width, count):
-    narrow = width // 7 // 128 * 128
-    wide = (width - narrow) // count // 128 * 128
-    pieces = [(i * wide, wide, True) for i in range(count)]
-    return pieces, (count * wide, width - count * wide, False)
+def cuts(width, shares, narrow_count):
+    unit = width // 7 // 128 * 128
+    pieces, at = [], 0
+    for share in shares:
+        pieces.append((at, share * unit, True))
+        at += share * unit
+    step = (width - at) // narrow_count // 128 * 128
+    narrow = []
+    for i in range(narrow_count):
+        w = step if i < narrow_count - 1 else width - at
+        narrow.append((at, w, False))
+        at += w
+    return narrow + pieces
+
+
+def plan(width):
+    gather = cuts(width, (3, 3), 1)
+    return gather, (cuts(width, (2,), 2), cuts(width, (2, 2, 2), 1))
 
 
 def exchange(
     pipes,
-    wide_count,
     layer_ref,
     upstream_ref,
     gate_ref,
@@ -189,14 +202,14 @@
     above, below = me + COLS, me - COLS
     width = layer_ref.shape[1]
     total = x_all.shape[0]
-    wide, narrow = cuts(width, wide_count)
-    pieces = [narrow] + wide
+    pieces, sum_pieces = plan(width)
     count = len(pieces)
+    span = total // 2
     not_top, not_low = z < top, z > 0
     to_pipe, from_pipe = stage > 0, stage < pipes - 1
 
-    def rows(block):
-        return pl.ds(pl.multiple_of(block * CAP, CAP), CAP)
+    def rows(half, block):
+        return pl.ds(pl.multiple_of(half * span + block * HALF, HALF), HALF)
 
     local = []
 
@@ -277,46 +290,88 @@
             device_id_type=MESH,
         ).wait_recv()
 
-    messages = []
-    for array in (x_all, g_all):
-        for c, w, is_wide in pieces:
-            if array is g_all and not is_wide:
-                w = w + 128
-            messages.append((array, c, w, is_wide, len(messages)))
+    messages = ([], [])
+    number = 0
+    for half in range(2):
+        for array in (x_all, g_all):
+            for c, w, is_wide in pieces:
+                if array is g_all and c + w == width:
+                    w = w + 128
+                messages[half].append((half, array, c, w, is_wide, number))
+                number += 1
 
     def gather_send(message, block, conds, tx, device):
-        array, c, w, _, n = message
-        view = lambda: array.at[rows(block), pl.ds(c, w)]
-        return send(
-            conds, view, view, lambda: tx.at[block, n], lambda: ag_rx.at[block, n], device
+        half, array, c, w, _, n = message
+        view = lambda: array.at[rows(half, block), pl.ds(c, w)]
+        sent.append(
+            send(conds, view, view, lambda: tx.at[block, n], lambda: ag_rx.at[block, n], device)
         )
 
     def gather_wait(message, block):
-        array, c, w, _, n = message
-        arrived(array.at[rows(block), pl.ds(c, w)], ag_y.at[block, n], ag_rx.at[block, n])
+        half, array, c, w, _, n = message
+        view = array.at[rows(half, block), pl.ds(c, w)]
+        arrived(view, ag_y.at[block, n], ag_rx.at[block, n])
 
     to_above = {"expert": above}
     to_below = {"expert": below}
     to_partner = {"expert": partner}
+    to_prev = {"pipe": stage - 1}
+    beside = z * COLS + other
+
+    def own(half, conds, tx, device):
+        for message in messages[half]:
+            gather_send(message, me, conds, tx, device)
+
+    def narrow_beside(half):
+        for message in messages[half]:
+            if not message[4]:
+                gather_wait(message, beside)
+
+    def pass_beside(half, conds, tx, device):
+        for message in messages[half]:
+            if not message[4]:
+                gather_send(message, beside, conds, tx, device)
+
+    def gather_stage(half, k):
+        for message in messages[half]:
+            for low in (True, False):
+                at_z = z - k if low else z + k
+                valid = z >= k if low else z + k <= top
+                onward, tx, device = (
+                    (not_top, ag_up, to_above) if low else (not_low, ag_dn, to_below)
+                )
+                for column in [y] if message[4] else [y, other]:
+                    block = at_z * COLS + column
+                    guard([valid], functools.partial(gather_wait, message, block))
+                    gather_send(message, block, [valid, onward], tx, device)
+                    if message[4]:
+                        gather_send(message, block, [valid], ag_y, to_partner)
+
+    def gather_end(half):
+        for message in messages[half]:
+            if message[4]:
+                for at_z in range(top + 1):
+                    gather_wait(message, at_z * COLS + other)
 
     picked = select_ref[...]
-    g_all[rows(me), pl.ds(width, 128)] = weight_ref[...]
-    for message in messages:
-        array, c, w, is_wide, n = message
+    for half in range(2):
+        g_all[rows(half, me), pl.ds(width, 128)] = weight_ref[pl.ds(half * HALF, HALF), :]
+    for first, second in zip(*messages):
+        _, array, c, _, _, n = first
         at = n % count
         loads, source = (
             (layer_loads, layer_buf) if array is x_all else (upstream_loads, upstream_buf)
         )
-        span = pieces[at][1]
+        w = pieces[at][1]
         loads[at].wait()
-        array[rows(me), pl.ds(c, span)] = jnp.dot(
-            picked, source[:, pl.ds(c, span)], preferred_element_type=jnp.float32
+        chosen = jnp.dot(
+            picked, source[:, pl.ds(c, w)], preferred_element_type=jnp.float32
         ).astype(jnp.bfloat16)
-        sent.append(gather_send(message, me, [], ag_y, to_partner))
-        sent.append(gather_send(message, me, [not_top], ag_up, to_above))
-        sent.append(gather_send(message, me, [not_low], ag_dn, to_below))
-
-    to_prev = {"pipe": stage - 1}
+        array[rows(0, me), pl.ds(c, w)] = chosen[:HALF]
+        array[rows(1, me), pl.ds(c, w)] = chosen[HALF:]
+        gather_send(first, me, [], ag_y, to_partner)
+        gather_send(first, me, [not_top], ag_up, to_above)
+        gather_send(first, me, [not_low], ag_dn, to_below)
     sent.append(
         send(
             [to_pipe],
@@ -338,173 +393,190 @@
         )
     )
 
-    beside = z * COLS + other
-    for message in messages:
-        if not message[3]:
-            gather_wait(message, beside)
-            sent.append(gather_send(message, beside, [not_top], ag_up, to_above))
-            sent.append(gather_send(message, beside, [not_low], ag_dn, to_below))
-
+    narrow_beside(0)
+    pass_beside(0, [not_top], ag_up, to_above)
+    pass_beside(0, [not_low], ag_dn, to_below)
+    own(1, [not_low, z == top], ag_dn, to_below)
+    own(1, [not_top, z == 0], ag_up, to_above)
     for k in range(1, top + 1):
-        for message in messages:
+        gather_stage(0, k)
+        if k < top:
+            own(1, [z == top - k], ag_dn, to_below)
+            own(1, [z == k], ag_up, to_above)
+    own(1, [], ag_y, to_partner)
+    narrow_beside(1)
+    pass_beside(1, [not_top], ag_up, to_above)
+    pass_beside(1, [not_low], ag_dn, to_below)
+
+    step = width // 7
+
+    def layer(half):
+        mine = pl.ds(half * span, span)
+        both[...] = jnp.zeros_like(both)
+        back[...] = jnp.zeros_like(back)
+
+        def forward(i, _):
+            at = pl.ds(pl.multiple_of(i * step, 128), step)
+            both[...] += jnp.dot(x_all[mine, at], w_pair[at, :], preferred_element_type=jnp.float32)
+            back[...] += lax.dot_general(
+                g_all[mine, at],
+                w_down[:, at],
+                (((1,), (1,)), ((), ())),
+                preferred_element_type=jnp.float32,
+            )
+            return 0
+
+        lax.fori_loop(0, 7, forward, 0)
+        gate = both[:, pl.ds(0, 128)]
+        up = both[:, pl.ds(128, 128)]
+        raw = back[...]
+        scale = g_all[mine, pl.ds(width, 128)].astype(jnp.float32)
+        sigmoid = jax.nn.sigmoid(gate)
+        silu = gate * sigmoid
+        hidden = (silu * up).astype(jnp.bfloat16).astype(jnp.float32)
+        score = jnp.sum(hidden * raw, axis=1, keepdims=True)
+        part[mine, pl.ds(width, 128)] = jnp.broadcast_to(score, (span, 128)).astype(jnp.bfloat16)
+        scaled = scale * raw
+        pair_out[mine, pl.ds(0, 128)] = (
+            scaled * up * sigmoid * (1.0 + gate * (1.0 - sigmoid))
+        ).astype(jnp.bfloat16)
+        pair_out[mine, pl.ds(128, 128)] = (scaled * silu).astype(jnp.bfloat16)
+        hidden_out[mine, :] = (hidden * scale).astype(jnp.bfloat16)
+
+    sum_count = max(len(p) for p in sum_pieces)
+
+    def sum_piece(half, n):
+        c, w, is_wide = sum_pieces[half][n]
+        return c, w + 128 if c + w == width else w, is_wide
+
+    def part_view(buffer, half, n, block):
+        c, w, _ = sum_piece(half, n)
+        return buffer.at[rows(half, block), pl.ds(c, w)]
+
+    def part_send(half, n, block, conds, buffer, tx, rx, device):
+        at = half * sum_count + n
+        sent.append(
+            send(
+                conds,
+                lambda: part_view(part, half, n, block),
+                lambda: part_view(buffer, half, n, block),
+                lambda: tx.at[block, at],
+                lambda: rx.at[block, at],
+                device,
+            )
+        )
+
+    def part_wait(half, n, block, buffer, tx, rx):
+        at = half * sum_count + n
+        arrived(part_view(buffer, half, n, block), tx.at[block, at], rx.at[block, at])
+
+    def back_rows(half):
+        mine = pl.ds(half * span, span)
+        for n, (c, w, is_wide) in enumerate(sum_pieces[half]):
+            for start in range(c, c + w, 1024):
+                at = pl.ds(start, min(1024, c + w - start))
+                part[mine, at] = lax.dot_general(
+                    pair_out[mine, :],
+                    w_pair[at, :],
+                    (((1,), (1,)), ((), ())),
+                    preferred_element_type=jnp.float32,
+                ).astype(jnp.bfloat16)
+            if is_wide:
+                for k in range(top, 0, -1):
+                    for at_z, valid in ((z - k, z >= k), (z + k, z + k <= top)):
+                        block = at_z * COLS + other
+                        part_send(half, n, block, [valid], from_y, rs_y_tx, rs_y_rx, to_partner)
+                part_send(half, n, beside, [], from_y, rs_y_tx, rs_y_rx, to_partner)
+
+    def merge(half, n, block, terms):
+        c, w, _ = sum_piece(half, n)
+        here = (rows(half, block), pl.ds(c, w))
+        temp[:, pl.ds(0, w)] = part[here].astype(jnp.float32)
+        for cond, buffer, tx, rx in terms:
+
+            def add(buffer=buffer, tx=tx, rx=rx):
+                part_wait(half, n, block, buffer, tx, rx)
+                temp[:, pl.ds(0, w)] += buffer[here].astype(jnp.float32)
+
+            guard([] if cond is None else [cond], add)
+        part[here] = temp[:, pl.ds(0, w)].astype(jnp.bfloat16)
+
+    via_y = (None, from_y, rs_y_tx, rs_y_rx)
+    via_above = (not_top, from_above, rs_dn_tx, rs_dn_rx)
+    via_below = (not_low, from_below, rs_up_tx, rs_up_rx)
+
+    def sum_stage(half, k):
+        for n, (_, _, is_wide) in enumerate(sum_pieces[half]):
             for low in (True, False):
                 at_z = z - k if low else z + k
                 valid = z >= k if low else z + k <= top
-                onward, tx, device = (
-                    (not_top, ag_up, to_above) if low else (not_low, ag_dn, to_below)
-                )
-                for column in [y] if message[3] else [y, other]:
-                    block = at_z * COLS + column
-                    guard([valid], functools.partial(gather_wait, message, block))
-                    sent.append(gather_send(message, block, [valid, onward], tx, device))
-                    if message[3]:
-                        sent.append(gather_send(message, block, [valid], ag_y, to_partner))
-    for message in messages:
-        if message[3]:
-            for at_z in range(top + 1):
-                gather_wait(message, at_z * COLS + other)
-
-    for copy in weight_loads:
-        copy.wait()
-    rows_copy = load(x_all, rows_out)
-    grads_copy = load(g_all.at[:, pl.ds(0, width)], grads_out)
-    step = width // 7
-    both[...] = jnp.zeros_like(both)
-    back[...] = jnp.zeros_like(back)
-
-    def forward(i, _):
-        at = pl.ds(pl.multiple_of(i * step, 128), step)
-        both[...] += jnp.dot(x_all[:, at], w_pair[at, :], preferred_element_type=jnp.float32)
-        back[...] += lax.dot_general(
-            g_all[:, at],
-            w_down[:, at],
-            (((1,), (1,)), ((), ())),
-            preferred_element_type=jnp.float32,
-        )
-        return 0
-
-    lax.fori_loop(0, 7, forward, 0)
-    gate = both[:, pl.ds(0, 128)]
-    up = both[:, pl.ds(128, 128)]
-    raw = back[...]
-    scale = g_all[:, pl.ds(width, 128)].astype(jnp.float32)
-    sigmoid = jax.nn.sigmoid(gate)
-    silu = gate * sigmoid
-    hidden = (silu * up).astype(jnp.bfloat16).astype(jnp.float32)
-    score = jnp.sum(hidden * raw, axis=1, keepdims=True)
-    part[:, pl.ds(width, 128)] = jnp.broadcast_to(score, (total, 128)).astype(jnp.bfloat16)
-    scaled = scale * raw
-    pair_out[:, pl.ds(0, 128)] = (
-        scaled * up * sigmoid * (1.0 + gate * (1.0 - sigmoid))
-    ).astype(jnp.bfloat16)
-    pair_out[:, pl.ds(128, 128)] = (scaled * silu).astype(jnp.bfloat16)
-    hidden_out[...] = (hidden * scale).astype(jnp.bfloat16)
-
-    def part_view(buffer, block, n):
-        c, w, is_wide = pieces[n]
-        return buffer.at[rows(block), pl.ds(c, w if is_wide else w + 128)]
-
-    def part_send(n, block, conds, buffer, tx, rx, device):
-        return send(
-            conds,
-            lambda: part_view(part, block, n),
-            lambda: part_view(buffer, block, n),
-            lambda: tx.at[block, n],
-            lambda: rx.at[block, n],
-            device,
-        )
-
-    def part_wait(n, block, buffer, tx, rx):
-        arrived(part_view(buffer, block, n), tx.at[block, n], rx.at[block, n])
-
-    def order(run):
-        for k in range(top, 0, -1):
-            run(z - k, z >= k)
-            run(z + k, z + k <= top)
-        run(z, None)
-
-    for n, (c, w, is_wide) in enumerate(pieces):
-        for start in range(c, c + w, 1024):
-            at = pl.ds(start, min(1024, c + w - start))
-            part[:, at] = lax.dot_general(
-                pair_out[...],
-                w_pair[at, :],
-                (((1,), (1,)), ((), ())),
-                preferred_element_type=jnp.float32,
-            ).astype(jnp.bfloat16)
-        if is_wide:
-            order(
-                lambda at_z, valid, n=n: sent.append(
-                    part_send(
-                        n,
-                        at_z * COLS + other,
-                        [] if valid is None else [valid],
-                        from_y,
-                        rs_y_tx,
-                        rs_y_rx,
-                        to_partner,
-                    )
-                )
-            )
-
-    def merge(n, block, terms):
-        c, w, is_wide = pieces[n]
-        w = w if is_wide else w + 128
-        here = (rows(block), pl.ds(c, w))
-        temp[:, pl.ds(0, w)] = part[here].astype(jnp.float32)
-        for cond, buffer, tx, rx in terms:
-
-            def add(buffer=buffer, tx=tx, rx=rx):
-                part_wait(n, block, buffer, tx, rx)
-                temp[:, pl.ds(0, w)] += buffer[here].astype(jnp.float32)
-
-            guard([] if cond is None else [cond], add)
-        part[here] = temp[:, pl.ds(0, w)].astype(jnp.bfloat16)
-
-    via_y = (None, from_y, rs_y_tx, rs_y_rx)
-    via_above = (not_top, from_above, rs_dn_tx, rs_dn_rx)
-    via_below = (not_low, from_below, rs_up_tx, rs_up_rx)
-    for k in range(top, 0, -1):
-        for n in range(count):
-            for low in (True, False):
-                at_z = z - k if low else z + k
-                valid = z >= k if low else z + k <= top
-                is_wide = pieces[n][2]
                 for column in [y] if is_wide else [y, other]:
                     block = at_z * COLS + column
-                    terms = ([via_y] if is_wide else []) + [via_above if low else via_below]
-                    guard([valid], functools.partial(merge, n, block, terms))
+                    via_z, edge = (via_above, not_top) if low else (via_below, not_low)
+                    if is_wide:
+                        guard([valid], functools.partial(merge, half, n, block, [via_y, via_z]))
+                    else:
+                        only = [(None,) + via_z[1:]]
+                        guard([valid, edge], functools.partial(merge, half, n, block, only))
                     if low:
                         out = (from_above, rs_dn_tx, rs_dn_rx, to_below)
                     else:
                         out = (from_below, rs_up_tx, rs_up_rx, to_above)
-                    sent.append(part_send(n, block, [valid], *out))
-    for n in range(count):
-        c, w, is_wide = pieces[n]
-        if is_wide:
-            merge(n, me, [via_y, via_above, via_below])
-        else:
-            merge(n, beside, [via_above, via_below])
-            sent.append(part_send(n, beside, [], from_y, rs_y_tx, rs_y_rx, to_partner))
-            merge(n, me, [via_above, via_below, via_y])
-        sent.append(
-            send(
-                [to_pipe],
-                lambda c=c, w=w: part.at[rows(me), pl.ds(c, w)],
-                lambda c=c, w=w: sums_out.at[:, pl.ds(c, w)],
-                lambda n=n: pipe_tx.at[2 + n],
-                lambda n=n: pipe_rx.at[2 + n],
-                to_prev,
+                    part_send(half, n, block, [valid], *out)
+
+    def sum_end(half):
+        for n, (_, _, is_wide) in enumerate(sum_pieces[half]):
+            if not is_wide:
+                merge(half, n, beside, [via_above, via_below])
+                part_send(half, n, beside, [], from_y, rs_y_tx, rs_y_rx, to_partner)
+        for n, (c, w, is_wide) in enumerate(sum_pieces[half]):
+            merge(half, n, me, [via_above, via_below, via_y])
+            at = 2 + half * sum_count + n
+            sent.append(
+                send(
+                    [to_pipe],
+                    lambda c=c, w=w: part.at[rows(half, me), pl.ds(c, w)],
+                    lambda c=c, w=w: sums_out.at[pl.ds(half * HALF, HALF), pl.ds(c, w)],
+                    lambda at=at: pipe_tx.at[at],
+                    lambda at=at: pipe_rx.at[at],
+                    to_prev,
+                )
             )
+        score_out[pl.ds(half * HALF, HALF), :] = part[rows(half, me), pl.ds(width, 128)].astype(
+            jnp.float32
         )
-    score_out[...] = part[rows(me), pl.ds(width, 128)].astype(jnp.float32)
+
+    gather_stage(1, 1)
+    gather_end(0)
+    for copy in weight_loads:
+        copy.wait()
+    layer(0)
+    back_rows(0)
+    sum_stage(0, top)
+    gather_stage(1, 2)
+    sum_stage(0, 2)
+    gather_stage(1, 3)
+    sum_stage(0, 1)
+    gather_end(1)
+    rows_copy = load(x_all, rows_out)
+    grads_copy = load(g_all.at[:, pl.ds(0, width)], grads_out)
+    layer(1)
+    back_rows(1)
+    sum_stage(1, top)
+    sum_end(0)
+    sum_stage(1, 2)
+    sum_stage(1, 1)
+    sum_end(1)
 
     @pl.when(from_pipe)
     def _():
         arrived(select_out, pipe_tx.at[0], pipe_rx.at[0])
         arrived(behind_out, pipe_tx.at[1], pipe_rx.at[1])
-        for n, (c, w, _) in enumerate(pieces):
-            arrived(sums_out.at[:, pl.ds(c, w)], pipe_tx.at[2 + n], pipe_rx.at[2 + n])
+        for half in range(2):
+            for n, (c, w, _) in enumerate(sum_pieces[half]):
+                at = 2 + half * sum_count + n
+                view = sums_out.at[pl.ds(half * HALF, HALF), pl.ds(c, w)]
+                arrived(view, pipe_tx.at[at], pipe_rx.at[at])
 
     for conds, make in sent:
         guard(conds, lambda make=make: make().wait_send())
@@ -551,16 +623,16 @@
         jnp.where(hits, combine_weights[0].astype(jnp.float32).T[:, None, :], 0.0), axis=(0, 2)
     )
     weight = jnp.broadcast_to(weight.astype(half)[:, None], (CAP, 128))
-    wide_count = 3
-    wide, narrow = cuts(width, wide_count)
-    count = len(wide) + 1
-    widest = max([w for _, w, _ in wide] + [narrow[1] + 128])
+    pieces, sum_pieces = plan(width)
+    count = len(pieces)
+    sum_count = max(len(p) for p in sum_pieces)
+    widest = max(w for p in sum_pieces for _, w, _ in p) + 128
     dma = pltpu.SemaphoreType.DMA
     vmem = pl.BlockSpec(memory_space=pltpu.VMEM)
     hbm = pl.BlockSpec(memory_space=pl.ANY)
     shape = jax.ShapeDtypeStruct
     x_all, g_all, pair, hidden, behind, select_next, sums, score = pl.pallas_call(
-        functools.partial(exchange, pipes, wide_count),
+        functools.partial(exchange, pipes),
         out_shape=(
             shape((total, width), half),
             shape((total, width), half),
@@ -584,17 +656,17 @@
             pltpu.VMEM((total, width + 128), half),
             pltpu.VMEM((total, width + 128), half),
             pltpu.VMEM((total, width + 128), half),
-            pltpu.VMEM((total, 2 * units), jnp.float32),
-            pltpu.VMEM((total, units), jnp.float32),
-            pltpu.VMEM((CAP, widest), jnp.float32),
+            pltpu.VMEM((total // 2, 2 * units), jnp.float32),
+            pltpu.VMEM((total // 2, units), jnp.float32),
+            pltpu.VMEM((HALF, widest), jnp.float32),
             dma((2 * count + 5,)),
-            *[dma((GROUP, 2 * count)) for _ in range(4)],
-            *[dma((GROUP, count)) for _ in range(6)],
-            dma((2 + count,)),
-            dma((2 + count,)),
+            *[dma((GROUP, 4 * count)) for _ in range(4)],
+            *[dma((GROUP, 2 * sum_count)) for _ in range(6)],
+            dma((2 + 2 * sum_count,)),
+            dma((2 + 2 * sum_count,)),
         ],
         compiler_params=pltpu.CompilerParams(
-            collective_id=0, has_side_effects=True, vmem_limit_bytes=50 * 1024 * 1024
+            collective_id=0, has_side_effects=True, vmem_limit_bytes=60 * 1024 * 1024
         ),
         name="exchange",
     )(
@@ -631,7 +703,7 @@
             across(CAP),
         ],
         out_specs=(across(tokens), along, along, across(units)),
-        compiler_params=pltpu.CompilerParams(vmem_limit_bytes=40 * 1024 * 1024),
+        compiler_params=pltpu.CompilerParams(vmem_limit_bytes=60 * 1024 * 1024),
         name="finish",
     )(keep, x_all, g_all, pair, hidden, behind, select_next, sums)
     router_grad = jnp.sum(jnp.where(hits, score[:, 0][None, :, None], 0.0), axis=1).T

time: 162 us -> 148 us (0.914)
  Pallas kernels: 151 us -> 143 us
  local copies, waits for them, and re-layouts: 7.79 us -> 0.78 us
    pallas_call x1, Pallas kernels: 145 us -> 132 us  [fused(): pl.pallas_call(functools.partial(exchange, pipes), out_shape=(shape((tota...]
    unnamed x8 -> x2, local copies, waits for them, and re-layouts: 7.61 us -> 0.01 us
    pallas_call x1, Pallas kernels: 6.63 us -> 11.6 us  [fused(): pl.pallas_call(finish, grid=(7,), out_shape=(shape((tokens, width), half)...]
where the time goes in v2:
time: 148 us; the launch traced here: 147 us
  Pallas kernels  143 us (97%)
  other arithmetic  2.79 us (2%)
    pallas_call x1, Pallas kernels, fused(): pl.pallas_call(functools.partial(exchange, pipes), out_shape=(shape((tota...  132 us
    pallas_call x1, Pallas kernels, fused(): pl.pallas_call(finish, grid=(7,), out_shape=(shape((tokens, width), half)...  11.6 us

profile of v2, /device:TPU:17, one launch (start us, length us, event | category | flops | bytes accessed | tf_op | source)
XLA Modules:
  0.0 147.5 jit_solution(5265353224899099314)
XLA Ops:
  0.6 0.7 select_bitcast_fusion
  1.4 0.7 convert_bitcast_fusion
  2.0 0.7 select_reduce_fusion.1
  2.7 0.7 broadcast_in_dim.51.weight_ref
  3.4 131.7 %exchange.1 = (bf16[256,7168]{1,0:T(8,128)(2,1)}, bf16[256,7168]{1,0:T(8,128)(2,1)}, bf16[256,256]{1,0:T(8,128)(2,1)}, bf16[256,128]{1,0:T(8,128)(2,1)}, bf16[25...) custom-call(bf16[256,7168]{1,0:T(8,128)(2,1)} %bitcast.22, ...), custom_call_target="tpu_custom_call" | custom-call | tf_op jit(solution)/shard_map/exchange/pallas_call | solution.py:634
  135.0 0.0 copy-start
  135.0 11.6 %finish.1 = (bf16[256,7168]{1,0:T(8,128)(2,1)}, bf16[7168,128]{1,0:T(8,128)(2,1)}, bf16[7168,128]{1,0:T(8,128)(2,1)}, bf16[128,7168]{1,0:T(8,128)(2,1)}) custom-call(s32[1]{0:T(128)} %bitcast.keep, bf16[256,7168]{1,0:T(8,128)(2,1)} %get-tuple-element.17.x, bf16[256,7168]{1,0:T(8,128)(2,1)} %get-tuple-element.18.g, bf16[256,256]{1,0:T(8,128)(2,1)} %get-tuple-element.19.pair, ...), custom_call_target="tpu_custom_call" | custom-call | tf_op jit(solution)/shard_map/finish/pallas_call | solution.py:686
  146.6 0.0 copy-done
  146.6 0.1 slice_reduce_fusion
  146.8 0.7 select_reduce_fusion
Async XLA Ops:
  135.0 11.6 %copy-start = (f32[32,128]{1,0:T(8,128)S(1)}, f32[32,128]{1,0:T(8,128)}, u32[]{:S(2)}) copy-start(f32[32,128]{1,0:T(8,128)} %get-tuple-element.28) | copy-start | bytes 49156

commit v3 on v2

--- a/solution.py
+++ b/solution.py
@@ -148,6 +148,12 @@
     return gather, (cuts(width, (2,), 2), cuts(width, (2, 2, 2), 1))
 
 
+def hits_of(routes, places, k):
+    route, place = routes[pl.ds(k, 1), :], places[pl.ds(k, 1), :]
+    position = jnp.where((route < 1) & (place < CAP), route * CAP + place, CAP)
+    return position == lax.broadcasted_iota(jnp.int32, (CAP, routes.shape[1]), 0)
+
+
 def exchange(
     pipes,
     layer_ref,
@@ -155,8 +161,9 @@
     gate_ref,
     up_ref,
     down_ref,
-    select_ref,
-    weight_ref,
+    routes_ref,
+    places_ref,
+    combine_ref,
     rows_out,
     grads_out,
     pair_out,
@@ -165,6 +172,7 @@
     select_out,
     sums_out,
     score_out,
+    select_ref,
     layer_buf,
     upstream_buf,
     x_all,
@@ -231,6 +239,17 @@
         load(down_ref, w_down),
     ]
 
+    picked = jnp.zeros(select_ref.shape, jnp.float32)
+    weight = jnp.zeros(select_ref.shape, jnp.float32)
+    for k in range(routes_ref.shape[0]):
+        hit = hits_of(routes_ref, places_ref, k)
+        picked = picked + jnp.where(hit, 1.0, 0.0)
+        combine = combine_ref[pl.ds(k, 1), :].astype(jnp.float32)
+        weight = weight + jnp.where(hit, combine, 0.0)
+    select_ref[...] = picked.astype(jnp.bfloat16)
+    weight = jnp.broadcast_to(jnp.sum(weight, axis=1, keepdims=True), (CAP, 128))
+    weight = weight.astype(jnp.bfloat16)
+
     barrier = pltpu.get_barrier_semaphore()
     pl.semaphore_signal(barrier, inc=1, device_id={"expert": partner}, device_id_type=MESH)
 
@@ -355,7 +374,7 @@
 
     picked = select_ref[...]
     for half in range(2):
-        g_all[rows(half, me), pl.ds(width, 128)] = weight_ref[pl.ds(half * HALF, HALF), :]
+        g_all[rows(half, me), pl.ds(width, 128)] = weight[half * HALF : (half + 1) * HALF]
     for first, second in zip(*messages):
         _, array, c, _, _, n = first
         at = n % count
@@ -470,23 +489,39 @@
         at = half * sum_count + n
         arrived(part_view(buffer, half, n, block), tx.at[block, at], rx.at[block, at])
 
-    def back_rows(half):
+    def back_piece(half, n):
         mine = pl.ds(half * span, span)
-        for n, (c, w, is_wide) in enumerate(sum_pieces[half]):
-            for start in range(c, c + w, 1024):
-                at = pl.ds(start, min(1024, c + w - start))
-                part[mine, at] = lax.dot_general(
-                    pair_out[mine, :],
-                    w_pair[at, :],
-                    (((1,), (1,)), ((), ())),
-                    preferred_element_type=jnp.float32,
-                ).astype(jnp.bfloat16)
-            if is_wide:
-                for k in range(top, 0, -1):
-                    for at_z, valid in ((z - k, z >= k), (z + k, z + k <= top)):
-                        block = at_z * COLS + other
-                        part_send(half, n, block, [valid], from_y, rs_y_tx, rs_y_rx, to_partner)
-                part_send(half, n, beside, [], from_y, rs_y_tx, rs_y_rx, to_partner)
+        c, w, _ = sum_pieces[half][n]
+        for start in range(c, c + w, 1024):
+            at = pl.ds(start, min(1024, c + w - start))
+            part[mine, at] = lax.dot_general(
+                pair_out[mine, :],
+                w_pair[at, :],
+                (((1,), (1,)), ((), ())),
+                preferred_element_type=jnp.float32,
+            ).astype(jnp.bfloat16)
+
+    def over_y(half, n, k):
+        if k == 0:
+            part_send(half, n, beside, [], from_y, rs_y_tx, rs_y_rx, to_partner)
+        else:
+            for at_z, valid in ((z - k, z >= k), (z + k, z + k <= top)):
+                block = at_z * COLS + other
+                part_send(half, n, block, [valid], from_y, rs_y_tx, rs_y_rx, to_partner)
+
+    def back_narrow(half):
+        for n, (_, _, is_wide) in enumerate(sum_pieces[half]):
+            if not is_wide:
+                back_piece(half, n)
+
+    def back_wide(half):
+        wide = [n for n, p in enumerate(sum_pieces[half]) if p[2]]
+        for n in wide:
+            back_piece(half, n)
+            over_y(half, n, top)
+        for k in range(top - 1, -1, -1):
+            for n in wide:
+                over_y(half, n, k)
 
     def merge(half, n, block, terms):
         c, w, _ = sum_piece(half, n)
@@ -505,8 +540,10 @@
     via_above = (not_top, from_above, rs_dn_tx, rs_dn_rx)
     via_below = (not_low, from_below, rs_up_tx, rs_up_rx)
 
-    def sum_stage(half, k):
+    def sum_stage(half, k, kind):
         for n, (_, _, is_wide) in enumerate(sum_pieces[half]):
+            if is_wide != kind:
+                continue
             for low in (True, False):
                 at_z = z - k if low else z + k
                 valid = z >= k if low else z + k <= top
@@ -524,11 +561,13 @@
                         out = (from_below, rs_up_tx, rs_up_rx, to_above)
                     part_send(half, n, block, [valid], *out)
 
-    def sum_end(half):
+    def sum_beside(half):
         for n, (_, _, is_wide) in enumerate(sum_pieces[half]):
             if not is_wide:
                 merge(half, n, beside, [via_above, via_below])
                 part_send(half, n, beside, [], from_y, rs_y_tx, rs_y_rx, to_partner)
+
+    def sum_end(half):
         for n, (c, w, is_wide) in enumerate(sum_pieces[half]):
             merge(half, n, me, [via_above, via_below, via_y])
             at = 2 + half * sum_count + n
@@ -546,26 +585,37 @@
             jnp.float32
         )
 
+    narrow_kind, wide_kind = False, True
     gather_stage(1, 1)
     gather_end(0)
     for copy in weight_loads:
         copy.wait()
     layer(0)
-    back_rows(0)
-    sum_stage(0, top)
+    back_narrow(0)
+    sum_stage(0, top, narrow_kind)
+    back_wide(0)
     gather_stage(1, 2)
-    sum_stage(0, 2)
-    gather_stage(1, 3)
-    sum_stage(0, 1)
+    sum_stage(0, 2, narrow_kind)
+    sum_stage(0, top, wide_kind)
+    sum_stage(0, 1, narrow_kind)
+    gather_stage(1, top)
+    sum_stage(0, 2, wide_kind)
+    sum_stage(0, 1, wide_kind)
     gather_end(1)
     rows_copy = load(x_all, rows_out)
     grads_copy = load(g_all.at[:, pl.ds(0, width)], grads_out)
+    sum_beside(0)
     layer(1)
-    back_rows(1)
-    sum_stage(1, top)
+    back_narrow(1)
+    sum_stage(1, top, narrow_kind)
+    back_wide(1)
+    sum_stage(1, 2, narrow_kind)
+    sum_stage(1, top, wide_kind)
+    sum_stage(1, 1, narrow_kind)
+    sum_stage(1, 2, wide_kind)
+    sum_beside(1)
+    sum_stage(1, 1, wide_kind)
     sum_end(0)
-    sum_stage(1, 2)
-    sum_stage(1, 1)
     sum_end(1)
 
     @pl.when(from_pipe)
@@ -585,8 +635,29 @@
 
 
 def finish(
-    keep, x, g, pair, hidden, behind, select, sums, prev_out, gate_out, up_out, down_out
+    keep,
+    routes,
+    places,
+    score,
+    x,
+    g,
+    pair,
+    hidden,
+    behind,
+    select,
+    sums,
+    prev_out,
+    gate_out,
+    up_out,
+    down_out,
+    router_out,
 ):
+    @pl.when(pl.program_id(0) == 0)
+    def _():
+        for k in range(routes.shape[0]):
+            named = jnp.where(hits_of(routes, places, k), score[:, :1], 0.0)
+            router_out[pl.ds(k, 1), :] = jnp.sum(named, axis=0, keepdims=True)
+
     first = (((0,), (0,)), ((), ()))
     grads = lax.dot_general(x[...], pair[...], first, preferred_element_type=jnp.float32)
     gate_out[...] = grads[:, :128].astype(jnp.bfloat16)
@@ -614,15 +685,7 @@
     half = jnp.bfloat16
     units = gate_weight.shape[2]
     total = GROUP * CAP
-    routes, places = expert_ids[0], slots[0]
-    usable = (routes < 1) & (places < CAP)
-    positions = jnp.where(usable, routes * CAP + places, CAP)
-    hits = positions.T[:, None, :] == lax.broadcasted_iota(jnp.int32, (1, CAP, 1), 1)
-    select = jnp.sum(hits.astype(jnp.float32), axis=0).astype(half)
-    weight = jnp.sum(
-        jnp.where(hits, combine_weights[0].astype(jnp.float32).T[:, None, :], 0.0), axis=(0, 2)
-    )
-    weight = jnp.broadcast_to(weight.astype(half)[:, None], (CAP, 128))
+    routes, places, combine = expert_ids[0].T, slots[0].T, combine_weights[0].T
     pieces, sum_pieces = plan(width)
     count = len(pieces)
     sum_count = max(len(p) for p in sum_pieces)
@@ -643,9 +706,10 @@
             shape((CAP, width), half),
             shape((CAP, 128), jnp.float32),
         ),
-        in_specs=[hbm, hbm, hbm, hbm, hbm, vmem, vmem],
+        in_specs=[hbm, hbm, hbm, hbm, hbm, vmem, vmem, vmem],
         out_specs=(hbm, hbm, vmem, vmem, hbm, hbm, hbm, vmem),
         scratch_shapes=[
+            pltpu.VMEM((CAP, tokens), half),
             pltpu.VMEM((tokens, width), half),
             pltpu.VMEM((tokens, width), half),
             pltpu.VMEM((total, width), half),
@@ -675,25 +739,31 @@
         gate_weight[0],
         up_weight[0],
         down_weight[0],
-        select,
-        weight,
+        routes,
+        places,
+        combine,
     )
     keep = jnp.where(lax.axis_index("pipe") < pipes - 1, 1, 0).astype(jnp.int32).reshape(1)
-    tile = width // 7
+    steps = 14
+    tile = width // steps
     across = lambda height: pl.BlockSpec((height, tile), lambda i: (0, i))
     along = pl.BlockSpec((tile, units), lambda i: (i, 0))
     whole = lambda *dims: pl.BlockSpec(dims, lambda i: (0, 0))
-    prev, gate_grad, up_grad, down_grad = pl.pallas_call(
+    prev, gate_grad, up_grad, down_grad, router = pl.pallas_call(
         finish,
-        grid=(7,),
+        grid=(steps,),
         out_shape=(
             shape((tokens, width), half),
             shape((width, units), half),
             shape((width, units), half),
             shape((units, width), half),
+            shape(routes.shape, jnp.float32),
         ),
         in_specs=[
             pl.BlockSpec(memory_space=pltpu.SMEM),
+            whole(*routes.shape),
+            whole(*routes.shape),
+            whole(CAP, 128),
             across(total),
             across(total),
             whole(total, 2 * units),
@@ -702,12 +772,11 @@
             whole(CAP, tokens),
             across(CAP),
         ],
-        out_specs=(across(tokens), along, along, across(units)),
+        out_specs=(across(tokens), along, along, across(units), whole(*routes.shape)),
         compiler_params=pltpu.CompilerParams(vmem_limit_bytes=60 * 1024 * 1024),
         name="finish",
-    )(keep, x_all, g_all, pair, hidden, behind, select_next, sums)
-    router_grad = jnp.sum(jnp.where(hits, score[:, 0][None, :, None], 0.0), axis=1).T
-    return (prev[None], gate_grad[None], up_grad[None], down_grad[None], router_grad[None])
+    )(keep, routes, places, score, x_all, g_all, pair, hidden, behind, select_next, sums)
+    return (prev[None], gate_grad[None], up_grad[None], down_grad[None], router.T[None])
 
 
 def solution(mesh):

time: 148 us -> 135 us (0.912)
  Pallas kernels: 143 us -> 133 us
  other arithmetic: 2.79 us -> 0 us
    pallas_call x1, Pallas kernels: 132 us -> 120 us  [fused(): pl.pallas_call(functools.partial(exchange, pipes), out_shape=(shape((tota...]
    pallas_call x1, Pallas kernels: 11.6 us -> 13.5 us  [fused(): pl.pallas_call(finish, grid=(steps,), out_shape=(shape((tokens, width), h...]
where the time goes in v3:
time: 135 us; the launch traced here: 134 us
  Pallas kernels  133 us (99%)
    pallas_call x1, Pallas kernels, fused(): pl.pallas_call(functools.partial(exchange, pipes), out_shape=(shape((tota...  120 us
    pallas_call x1, Pallas kernels, fused(): pl.pallas_call(finish, grid=(steps,), out_shape=(shape((tokens, width), h...  13.5 us

profile of v3, /device:TPU:17, one launch (start us, length us, event | category | flops | bytes accessed | tf_op | source)
XLA Modules:
  0.0 133.7 jit_solution(7378252102358734199)
XLA Ops:
  0.6 119.6 %exchange.1 = (bf16[256,7168]{1,0:T(8,128)(2,1)}, bf16[256,7168]{1,0:T(8,128)(2,1)}, bf16[256,256]{1,0:T(8,128)(2,1)}, bf16[256,128]{1,0:T(8,128)(2,1)}, bf16[25...) custom-call(bf16[256,7168]{1,0:T(8,128)(2,1)} %bitcast.22, ...), custom_call_target="tpu_custom_call" | custom-call | tf_op jit(solution)/shard_map/exchange/pallas_call | solution.py:697
  120.2 13.5 %finish.1 = (bf16[256,7168]{1,0:T(8,128)(2,1)}, bf16[7168,128]{1,0:T(8,128)(2,1)}, bf16[7168,128]{1,0:T(8,128)(2,1)}, bf16[128,7168]{1,0:T(8,128)(2,1)}, f32[8,256]{1,0:T(8,128)}) custom-call(s32[1]{0:T(128)} %bitcast.keep, s32[8,256]{1,0:T(8,128)} %bitcast.28, s32[8,256]{1,0:T(8,128)} %bitcast.30, f32[32,128]{1,0:T(8,128)} %get-tuple-element.18.score, ...), custom_call_target="tpu_custom_call" | custom-call | tf_op jit(solution)/shard_map/finish/pallas_call | solution.py:752
